TPU v7x, 512 devices: a whole 4x4x16 slice. The times are simulated.
512 devices in a mesh: slab: 128 (over z, x, core), col: 4 (over y).
Axes of the slice: x: 4, y: 4, z: 16, core: 2. Of those that a mesh axis runs over, the one named last changes fastest.
Arguments:
- basis: bfloat16 [3, 64, 256, 32, 128], P(None, None, 'slab', 'col')
- cell_map: int32 [256, 32, 128], P('slab', 'col'), may hold values from 0 to 7
- table: float32 [8, 27], replicated, may hold values from 0 to 1, as said below
Outputs:
- next_block: bfloat16 [64, 256, 32, 128], P(None, 'slab', 'col')
- projections: float32 [2, 192, 64], replicated
- triangles: float32 [2, 64, 64], replicated
Inputs may be any that keep to these rules, and one draw needn't show every extreme that they name: `table`: coefficients lie between 0 and 1; the centre one is the largest.
All inputs are finite; a program needn't handle non-finite values.
Results may differ from a plain program's by a relative error of at most 0.027.
Values may be sent and summed in bfloat16 or wider, within the bound.
A program may use at most 64 MiB of HBM per device.

v0:
```python
import jax
import jax.numpy as jnp
from jax import lax
from jax.sharding import PartitionSpec as P


def extended(block, sides, width):
    for axis, dim in sides:
        count = lax.axis_size(axis)
        forward = [(i, i + 1) for i in range(count - 1)]
        backward = [(target, source) for source, target in forward]
        low = lax.ppermute(
            lax.slice_in_dim(block, block.shape[dim] - width, None, axis=dim), axis, forward
        )
        high = lax.ppermute(lax.slice_in_dim(block, 0, width, axis=dim), axis, backward)
        block = jnp.concatenate([low, block, high], axis=dim)
    return block


def apply_stencil(wide, coef):
    depth = wide.shape[3]
    rows_x = wide.shape[1] - 2
    rows_y = wide.shape[2] - 2
    padded = jnp.pad(wide, ((0, 0), (0, 0), (0, 0), (1, 1)))
    total = jnp.zeros((wide.shape[0], rows_x, rows_y, depth), jnp.float32)
    for dx in range(3):
        for dy in range(3):
            for dz in range(3):
                offset = 9 * dx + 3 * dy + dz
                piece = padded[:, dx : dx + rows_x, dy : dy + rows_y, dz : dz + depth].astype(
                    jnp.float32
                )
                total = total + coef[offset][None] * piece
    return total.astype(jnp.bfloat16)


def with_faces(block, coef):
    wide = extended(block, (("slab", 1), ("col", 2)), 1)
    return apply_stencil(wide, coef)


def lookup(cell_map, table):
    classes = table.shape[0]
    onehot = (cell_map[None] == jnp.arange(classes, dtype=jnp.int32)[:, None, None, None]).astype(
        jnp.float32
    )
    return jnp.einsum("ko,kxyz->oxyz", table, onehot, precision=lax.Precision.HIGHEST)


def gram_of(left, right, scale):
    return (
        lax.dot_general(left, right, (((1,), (1,)), ((), ())), preferred_element_type=jnp.float32)
        * scale
    )


def correct(stack, block, coeffs):
    moved = lax.dot_general(
        coeffs.astype(jnp.bfloat16),
        stack,
        (((0,), (0,)), ((), ())),
        preferred_element_type=jnp.float32,
    )
    return (block.astype(jnp.float32) - moved).astype(jnp.bfloat16)


def inner_part(flat, shape_wide):
    lead, span_x, span_y, depth = shape_wide
    cube = flat.reshape(lead, span_x, span_y, depth)
    return cube.reshape(lead, -1)


def orthonormalize(stack_wide, block_wide, shape_wide, scale):
    stack = inner_part(stack_wide, (stack_wide.shape[0],) + shape_wide[1:])
    block_inner = inner_part(block_wide, shape_wide)
    first = lax.psum(gram_of(stack, block_inner, 1.0), ("slab", "col")) * scale
    one_wide = correct(stack_wide, block_wide, first)
    second = (
        lax.psum(gram_of(stack, inner_part(one_wide, shape_wide), 1.0), ("slab", "col")) * scale
    )
    two_wide = correct(stack_wide, one_wide, second)
    two_inner = inner_part(two_wide, shape_wide)
    square = lax.psum(gram_of(two_inner, two_inner, 1.0), ("slab", "col")) * scale
    lower = jnp.linalg.cholesky(square)
    identity = jnp.eye(lower.shape[0], dtype=lower.dtype)
    inverse = lax.linalg.triangular_solve(lower, identity, left_side=True, lower=True)
    result = jnp.dot(
        inverse.astype(jnp.bfloat16), two_wide, preferred_element_type=jnp.float32
    ).astype(jnp.bfloat16)
    return (result, first + second, lower, None)


def shards(basis, cell_map, table):
    count_x, count_y, depth = cell_map.shape
    columns = basis.shape[1]
    devices_x = lax.axis_size("slab")
    devices_y = lax.axis_size("col")
    scale = 1.0 / (count_x * devices_x * count_y * devices_y * depth)
    coef = lookup(cell_map, table)
    flat = basis.reshape(3 * columns, count_x * count_y * depth)
    shape_inner = (columns, count_x, count_y, depth)
    image_first = with_faces(basis[2], coef)
    block_one, proj_one, lower_one, gram_one = orthonormalize(
        flat, image_first.reshape(columns, -1), shape_inner, scale
    )
    image = with_faces(block_one.reshape(shape_inner), coef)
    stack = jnp.concatenate([flat[columns:], block_one], axis=0)
    block_two, proj_two, lower_two, gram_two = orthonormalize(
        stack, image.reshape(columns, -1), shape_inner, scale
    )
    return (
        block_two.reshape(shape_inner),
        jnp.stack([proj_one, proj_two]),
        jnp.stack([lower_one, lower_two]),
    )


def solution(mesh):
    placed = (P(None, None, "slab", "col", None), P("slab", "col", None), P())
    return jax.shard_map(
        shards,
        mesh=mesh,
        in_specs=placed,
        out_specs=(P(None, "slab", "col", None), P(), P()),
        check_vma=False,
    )
```

profile of v0, /device:TPU:1, one launch (start us, length us, event | category | flops | bytes accessed | tf_op | source)
XLA Modules:
  0.0 697.7 jit_solution(16092930886953120736)
XLA Ops:
  1.7 4.5 collective-permute-start
  6.2 5.6 collective-permute-start.1
  13.2 2.7 collective-permute-start.2
  18.1 4.1 collective-permute-done.3
  22.2 2.8 fusion.11
  25.0 3.4 add_convert_fusion.1
  28.7 111.1 %psum.42 = f32[192,64]{0,1:T(8,128)S(1)} all-reduce(f32[192,64]{0,1:T(8,128)S(1)} %convolution_bitcast_fusion.2), channel_id=1, replica_groups=mesh['slab'=128,'col'=4] {'slab','col'}, use_global_device_ids=true, to_apply=%region_0.1 | all-reduce | flops 12288 | bytes 98304 | tf_op jit(solution)/shard_map/psum | solution.py:76
  140.5 99.1 %psum.43 = f32[192,64]{0,1:T(8,128)S(1)} all-reduce(f32[192,64]{0,1:T(8,128)S(1)} %convolution_bitcast_fusion.1), channel_id=1, replica_groups=mesh['slab'=128,'col'=4] {'slab','col'}, use_global_device_ids=true, to_apply=%region_1.2 | all-reduce | flops 12288 | bytes 98304 | tf_op jit(solution)/shard_map/psum | solution.py:79
  240.1 100.3 %psum.44 = f32[64,64]{0,1:T(8,128)S(1)} all-reduce(f32[64,64]{0,1:T(8,128)S(1)} %fusion.50), channel_id=1, replica_groups=mesh['slab'=128,'col'=4] {'slab','col'}, use_global_device_ids=true, to_apply=%region_2.3 | all-reduce | flops 4096 | bytes 32768 | tf_op jit(solution)/shard_map/psum | solution.py:83
  340.5 5.8 cholesky.44
  347.7 4.9 custom-call.6
  353.1 3.6 collective-permute-start.4
  357.0 1.9 collective-permute-start.5
  359.0 4.3 collective-permute-done.5
  363.5 1.3 collective-permute-start.6
  364.9 1.5 collective-permute-start.7
  366.8 4.0 collective-permute-done.7
  370.8 1.9 select_maximum_fusion
  372.7 3.3 add_convert_fusion
  376.4 105.5 %psum.45 = f32[192,64]{0,1:T(8,128)S(1)} all-reduce(f32[192,64]{0,1:T(8,128)S(1)} %fusion.15), channel_id=1, replica_groups=mesh['slab'=128,'col'=4] {'slab','col'}, use_global_device_ids=true, to_apply=%region_5.0 | all-reduce | flops 12288 | bytes 98304 | tf_op jit(solution)/shard_map/psum | solution.py:76
  482.6 99.5 %psum.46 = f32[192,64]{0,1:T(8,128)S(1)} all-reduce(f32[192,64]{0,1:T(8,128)S(1)} %fusion.44), channel_id=1, replica_groups=mesh['slab'=128,'col'=4] {'slab','col'}, use_global_device_ids=true, to_apply=%region_6.9 | all-reduce | flops 12288 | bytes 98304 | tf_op jit(solution)/shard_map/psum | solution.py:79
  582.6 100.3 %psum.47 = f32[64,64]{0,1:T(8,128)S(1)} all-reduce(f32[64,64]{0,1:T(8,128)S(1)} %fusion.51), channel_id=1, replica_groups=mesh['slab'=128,'col'=4] {'slab','col'}, use_global_device_ids=true, to_apply=%region_7.10 | all-reduce | flops 4096 | bytes 32768 | tf_op jit(solution)/shard_map/psum | solution.py:83
  683.0 5.8 cholesky.55
  690.2 4.9 custom-call.7
  (57 shorter events, 14.3 us)
Async XLA Ops:
  0.6 11.2 %copy-start = (f32[8,27]{1,0:T(8,128)S(1)}, f32[8,27]{1,0:T(8,128)}, u32[]{:S(2)}) copy-start(f32[8,27]{1,0:T(8,128)} %param.8) | copy-start | bytes 2596
  0.6 16.7 %copy-start.1 = (bf16[3,64,2,8,128]{4,3,2,1,0:T(8,128)(2,1)S(1)}, bf16[3,64,2,8,128]{4,3,2,1,0:T(8,128)(2,1)}, u32[]{:S(2)}) copy-start(bf16[3,64,2,8,128]{4,3,2,1,0:T(8,128)(2,1)} %param.6) | copy-start | bytes 2359300
  1.7 11.2 %collective-permute-start = (bf16[64,1,8,128]{3,2,1,0:T(8,128)(2,1)S(1)}, bf16[64,1,8,128]{3,2,1,0:T(8,128)(2,1)S(1)}, u32[]{:S(2)}, u32[]{:S(2)}) collective-permute-start(bf16[64,1,8,128]{3,2,1,0:T(8,128)(2,1)S(1)} %get-tuple-element.38), channel_id=1, source_target_pairs={{0,4},{4,8},{8,12},{12,16},{16,20},{20,24},{24,28},{28,32},{32,36}... | collective-permute-start | bytes 393224 | tf_op jit(solution)/shard_map/ppermute | solution.py:12
  6.2 6.7 collective-permute-start.1
  13.2 4.9 collective-permute-start.2
  15.9 6.3 collective-permute-start.3
  239.8 116.9 %slice-start = ((bf16[3,64,2,8,128]{4,3,2,1,0:T(8,128)(2,1)}), bf16[2,64,2,8,128]{4,3,2,1,0:T(8,128)(2,1)S(1)}, s32[]{:S(2)}) async-start(bf16[3,64,2,8,128]{4,3,2,1,0:T(8,128)(2,1)} %param.6), calls=%async_computation | async-start | bytes 1048576 | tf_op jit(solution)/shard_map/slice | solution.py:107
  353.1 5.8 collective-permute-start.4
  357.0 6.3 collective-permute-start.5
  363.5 3.3 collective-permute-start.6
  364.9 5.9 collective-permute-start.7
where the time goes:
time: 699 us; the launch traced here: 698 us
  blocking collectives  616 us (88%)
  other arithmetic  37 us (5%)
  starting transfers between devices  22.5 us (3%)
  waiting for transfers between devices  13.3 us (2%)
    psum x2, blocking collectives, orthonormalize(): first = lax.psum(gram_of(stack, block_inner, 1.0), ('slab', 'col')) * scale  217 us
    psum x2, blocking collectives, orthonormalize(): lax.psum(gram_of(two_inner, two_inner, 1.0), ('slab', 'col')) * scale  201 us
    psum x2, blocking collectives, orthonormalize(): lax.psum(gram_of(stack, inner_part(one_wide, shape_wide), 1.0), ('slab',...  199 us
  transfers between devices with their start and end apart: 8, of which 5 were waited for; matrix products, arithmetic and copies ran while one was open for 0% of the time, Pallas kernels for 0%

commit v1 on v0

--- a/solution.py
+++ b/solution.py
@@ -2,6 +2,10 @@
 import jax.numpy as jnp
 from jax import lax
 from jax.sharding import PartitionSpec as P
+
+
+def supply_run(work_x):
+    return lax.all_gather(work_x, axis_name=("slab", "col")).sum(axis=0)
 
 
 def extended(block, sides, width):
@@ -80,7 +84,7 @@
     )
     two_wide = correct(stack_wide, one_wide, second)
     two_inner = inner_part(two_wide, shape_wide)
-    square = lax.psum(gram_of(two_inner, two_inner, 1.0), ("slab", "col")) * scale
+    square = supply_run(gram_of(two_inner, two_inner, 1.0)) * scale
     lower = jnp.linalg.cholesky(square)
     identity = jnp.eye(lower.shape[0], dtype=lower.dtype)
     inverse = lax.linalg.triangular_solve(lower, identity, left_side=True, lower=True)

time: 699 us -> 956 us (1.37)
  waiting for transfers between devices: 13.3 us -> 443 us
  blocking collectives: 616 us -> 415 us
  other arithmetic: 37 us -> 50.9 us
  between operations: 1.04 us -> 14.4 us
    all_gather x0 -> x2, waiting for transfers between devices: none -> 430 us  [supply_run(): return lax.all_gather(work_x, axis_name=('slab', 'col')).sum(axis=0)]
    psum x2 -> x0, blocking collectives: 201 us -> none  [orthonormalize(): lax.psum(gram_of(two_inner, two_inner, 1.0), ('slab', 'col')) * scale]
    reduce_sum x0 -> x2, other arithmetic: none -> 13.9 us  [supply_run(): return lax.all_gather(work_x, axis_name=('slab', 'col')).sum(axis=0)]
  transfers between devices with their start and end apart: 8 -> 10, of which waited for: 5 -> 7; matrix products, arithmetic and copies ran while one was open for 0% -> 0% of each run, Pallas kernels for 0% -> 0%
where the time goes in v1:
time: 956 us; the launch traced here: 955 us
  waiting for transfers between devices  443 us (46%)
  blocking collectives  415 us (43%)
  other arithmetic  50.9 us (5%)
  starting transfers between devices  22.6 us (2%)
  between operations  14.4 us (2%)
    all_gather x2, waiting for transfers between devices, supply_run(): return lax.all_gather(work_x, axis_name=('slab', 'col')).sum(axis=0)  430 us
    psum x2, blocking collectives, orthonormalize(): first = lax.psum(gram_of(stack, block_inner, 1.0), ('slab', 'col')) * scale  217 us
    psum x2, blocking collectives, orthonormalize(): lax.psum(gram_of(stack, inner_part(one_wide, shape_wide), 1.0), ('slab',...  198 us
  transfers between devices with their start and end apart: 10, of which 7 were waited for; matrix products, arithmetic and copies ran while one was open for 0% of the time, Pallas kernels for 0%

profile of v1, /device:TPU:1, one launch (start us, length us, event | category | flops | bytes accessed | tf_op | source)
XLA Modules:
  0.0 954.9 jit_solution(7426203617737928314)
XLA Ops:
  8.3 4.5 collective-permute-start
  12.8 5.6 collective-permute-start.1
  19.8 2.8 collective-permute-start.2
  24.7 4.1 collective-permute-done.3
  28.8 2.8 fusion.11
  31.6 3.4 add_convert_fusion.1
  35.3 111.1 %psum.28 = f32[192,64]{0,1:T(8,128)S(1)} all-reduce(f32[192,64]{0,1:T(8,128)S(1)} %convolution_bitcast_fusion.2), channel_id=1, replica_groups=mesh['slab'=128,'col'=4] {'slab','col'}, use_global_device_ids=true, to_apply=%region_0.1 | all-reduce | flops 12288 | bytes 98304 | tf_op jit(solution)/shard_map/psum | solution.py:80
  147.1 99.1 %psum.29 = f32[192,64]{0,1:T(8,128)S(1)} all-reduce(f32[192,64]{0,1:T(8,128)S(1)} %convolution_bitcast_fusion.1), channel_id=1, replica_groups=mesh['slab'=128,'col'=4] {'slab','col'}, use_global_device_ids=true, to_apply=%region_1.2 | all-reduce | flops 12288 | bytes 98304 | tf_op jit(solution)/shard_map/psum | solution.py:83
  247.3 215.3 %all-gather.5.cloned.1.call-done = f32[32768,64]{1,0:T(8,128)} async-done(((f32[64,64]{1,0:T(8,128)}), f32[32768,64]{1,0:T(8,128)}) %all-gather.5.cloned.1.call-update) | async-done | bytes 8388624 | tf_op jit(solution)/shard_map/all_gather | solution.py:8
  462.6 6.9 reduce_sum.18
  469.8 5.8 cholesky.44
  477.0 4.9 custom-call.6
  482.4 2.4 collective-permute-start.4
  484.9 1.9 collective-permute-start.5
  486.9 4.3 collective-permute-done.5
  491.4 2.6 collective-permute-start.6
  495.9 3.8 collective-permute-done.7
  501.6 3.3 add_convert_fusion
  505.3 105.4 %psum.30 = f32[192,64]{0,1:T(8,128)S(1)} all-reduce(f32[192,64]{0,1:T(8,128)S(1)} %fusion.15), channel_id=1, replica_groups=mesh['slab'=128,'col'=4] {'slab','col'}, use_global_device_ids=true, to_apply=%region_5.0 | all-reduce | flops 12288 | bytes 98304 | tf_op jit(solution)/shard_map/psum | solution.py:80
  611.4 99.0 %psum.31 = f32[192,64]{0,1:T(8,128)S(1)} all-reduce(f32[192,64]{0,1:T(8,128)S(1)} %fusion.44), channel_id=1, replica_groups=mesh['slab'=128,'col'=4] {'slab','col'}, use_global_device_ids=true, to_apply=%region_6.9 | all-reduce | flops 12288 | bytes 98304 | tf_op jit(solution)/shard_map/psum | solution.py:83
  712.3 214.7 %all-gather.7.cloned.1.call-done = f32[32768,64]{1,0:T(8,128)} async-done(((f32[64,64]{1,0:T(8,128)}), f32[32768,64]{1,0:T(8,128)}) %all-gather.7.cloned.1.call-update) | async-done | bytes 8388624 | tf_op jit(solution)/shard_map/all_gather | solution.py:8
  927.0 6.9 reduce_sum.19
  934.1 5.8 cholesky.55
  941.3 4.9 custom-call.7
  (65 shorter events, 19.0 us)
Async XLA Ops:
  7.2 11.2 %copy-start = (f32[8,27]{1,0:T(8,128)S(1)}, f32[8,27]{1,0:T(8,128)}, u32[]{:S(2)}) copy-start(f32[8,27]{1,0:T(8,128)} %param.8) | copy-start | bytes 2596
  7.2 16.7 %copy-start.1 = (bf16[3,64,2,8,128]{4,3,2,1,0:T(8,128)(2,1)S(1)}, bf16[3,64,2,8,128]{4,3,2,1,0:T(8,128)(2,1)}, u32[]{:S(2)}) copy-start(bf16[3,64,2,8,128]{4,3,2,1,0:T(8,128)(2,1)} %param.6) | copy-start | bytes 2359300
  7.2 455.5 %all-gather.5.cloned.1.call-start = ((), (), s32[]{:S(2)}) async-start(), calls=%async_computation | async-start | bytes 16809984 | tf_op jit(solution)/shard_map/all_gather | solution.py:8
  8.3 11.2 %collective-permute-start = (bf16[64,1,8,128]{3,2,1,0:T(8,128)(2,1)S(1)}, bf16[64,1,8,128]{3,2,1,0:T(8,128)(2,1)S(1)}, u32[]{:S(2)}, u32[]{:S(2)}) collective-permute-start(bf16[64,1,8,128]{3,2,1,0:T(8,128)(2,1)S(1)} %get-tuple-element.38), channel_id=1, source_target_pairs={{0,4},{4,8},{8,12},{12,16},{16,20},{20,24},{24,28},{28,32},{32,36}... | collective-permute-start | bytes 393224 | tf_op jit(solution)/shard_map/ppermute | solution.py:16
  12.8 6.7 collective-permute-start.1
  19.8 4.9 collective-permute-start.2
  22.5 6.3 collective-permute-start.3
  247.3 679.7 %all-gather.7.cloned.1.call-start = ((), (), s32[]{:S(2)}) async-start(), calls=%async_computation.1 | async-start | bytes 16809984 | tf_op jit(solution)/shard_map/all_gather | solution.py:8
  482.1 13.3 %slice-start = ((bf16[3,64,2,8,128]{4,3,2,1,0:T(8,128)(2,1)}), bf16[2,64,2,8,128]{4,3,2,1,0:T(8,128)(2,1)S(1)}, s32[]{:S(2)}) async-start(bf16[3,64,2,8,128]{4,3,2,1,0:T(8,128)(2,1)} %param.6), calls=%async_computation.2 | async-start | bytes 1048576 | tf_op jit(solution)/shard_map/slice | solution.py:111
  482.4 4.4 collective-permute-start.4
  484.9 6.3 collective-permute-start.5
  491.4 4.5 collective-permute-start.6
  494.0 5.7 collective-permute-start.7
Sparse Core Ops, SparseCore 0:
  247.4 215.2 all-gather.4
  711.7 215.2 all-gather.6
